TPU v7x, 32 devices: a whole 2x2x4 slice. The times are simulated.
32 devices in a mesh: rows: 8 (over z, y), cols: 4 (over x, core).
Axes of the slice: x: 2, y: 2, z: 4, core: 2. Of those that a mesh axis runs over, the one named last changes fastest.
Arguments:
- right_vecs: bfloat16 [2, 16384, 512], P(None, 'rows', 'cols'), may hold values from -6 to 6
- left_vecs: bfloat16 [2, 16384, 512], P(None, 'rows', 'cols'), may hold values from -0.0625 to 0.0625
- dip_blocks: bfloat16 [128, 8, 2, 128, 128], P('rows'), may hold values from -0.125 to 0.125
- block_cols: int32 [128, 8], P('rows'), may hold values from 0 to 127, as said below
- block_counts: int32 [128], P('rows'), may hold values from 1 to 8, as said below
Outputs:
- coupling: float32 [4, 128, 2, 512], P(None, 'rows')
Inputs may be any that keep to these rules, and one draw needn't show every extreme that they name: Block row r's columns lie within 16 blocks of r: |block_cols[r, j] - r| <= 16, slots at or past block_counts[r] included; such slots are not used. Slots in use fill the first block_counts[r] slots of a block row.
All inputs are finite; a program needn't handle non-finite values.
Results may differ from a plain program's by a relative error of at most 0.0029.
Values may be sent and summed in bfloat16 or wider, within the bound.
A program may use at most 128 MiB of HBM per device.

v0:
```python
import jax
import jax.numpy as jnp
from jax import lax
from jax.sharding import PartitionSpec as P


def padded(block, sides, width):
    for axis, dim in sides:
        count = lax.axis_size(axis)
        forward = [(i, i + 1) for i in range(count - 1)]
        backward = [(target, source) for source, target in forward]
        low = lax.ppermute(
            lax.slice_in_dim(block, block.shape[dim] - width, None, axis=dim), axis, forward
        )
        high = lax.ppermute(lax.slice_in_dim(block, 0, width, axis=dim), axis, backward)
        block = jnp.concatenate([low, block, high], axis=dim)
    return block


def inner_rows(first, second):
    return lax.dot_general(
        first, second, (((0,), (0,)), ((), ())), preferred_element_type=jnp.float32
    )


def project(left, right):
    real_part = inner_rows(left[0], right[0]) + inner_rows(left[1], right[1])
    imag_part = inner_rows(left[0], right[1]) - inner_rows(left[1], right[0])
    return jnp.stack([real_part, imag_part], axis=1)


def apply_blocks(mats, vecs):
    return jnp.einsum("ijpq,ijqk->ipk", mats, vecs, preferred_element_type=jnp.float32)


def local(right_vecs, left_vecs, dip_blocks, block_cols, block_counts):
    span = right_vecs.shape[1]
    width = right_vecs.shape[2]
    blocks_dev = dip_blocks.shape[0]
    slots = dip_blocks.shape[1]
    block_size = dip_blocks.shape[3]
    extended = padded(right_vecs, (("rows", 1),), span)
    stacked = extended.reshape(2, 3 * blocks_dev, block_size, width)
    first_block = (lax.axis_index("rows") - 1) * blocks_dev
    local_cols = block_cols - first_block
    picked = jnp.take(stacked, local_cols.reshape(-1), axis=1).reshape(
        2, blocks_dev, slots, block_size, width
    )
    valid = lax.broadcasted_iota(jnp.int32, (blocks_dev, slots), 1) < block_counts[:, None]
    picked = jnp.where(valid[None, :, :, None, None], picked, jnp.zeros_like(picked))
    dip_real = dip_blocks[:, :, 0]
    dip_imag = dip_blocks[:, :, 1]
    image_real = apply_blocks(dip_real, picked[0]) - apply_blocks(dip_imag, picked[1])
    image_imag = apply_blocks(dip_real, picked[1]) + apply_blocks(dip_imag, picked[0])
    image = jnp.stack([image_real, image_imag]).reshape(2, span, width).astype(jnp.bfloat16)
    groups = lax.axis_size("cols")
    partial_value = project(lax.all_gather(left_vecs, "cols", axis=2, tiled=True), image)
    partial_value = partial_value.reshape(groups, width, 2, width)
    shares = lax.psum_scatter(partial_value, "rows", scatter_dimension=1, tiled=True)
    return lax.all_gather(shares, "cols", axis=3, tiled=True)


def solution(mesh):
    in_specs = (
        P(None, "rows", "cols"),
        P(None, "rows", "cols"),
        P("rows", None, None, None, None),
        P("rows", None),
        P("rows"),
    )
    out_specs = P(None, "rows", None, None)
    return jax.shard_map(local, mesh=mesh, in_specs=in_specs, out_specs=out_specs, check_vma=False)
```

profile of v0, /device:TPU:0, one launch (start us, length us, event | category | flops | bytes accessed | tf_op | source)
XLA Modules:
  0.0 186.4 jit_solution(13700150421878237117)
XLA Ops:
  6.5 0.0 all-gather.2.cloned.1.call-start
  6.5 0.7 all-gather.2.cloned.1.call-update
  7.3 0.0 all-reduce.3.cloned.1.call-start
  7.3 4.9 %collective-permute-start = (bf16[2,2048,128]{2,1,0:T(8,128)(2,1)}, bf16[2,2048,128]{2,1,0:T(8,128)(2,1)S(1)}, u32[]{:S(2)}, u32[]{:S(2)}) collective-permute-start(bf16[2,2048,128]{2,1,0:T(8,128)(2,1)} %param.5), channel_id=1, source_target_pairs={{0,4},{4,8},{8,12},{12,16},{16,20},{20,24},{24,28},{1,5},{5,9},{9,... | collective-permute-start | bytes 3145736 | tf_op jit(solution)/shard_map/ppermute | solution.py:12
  12.2 1.3 collective-permute-start.1
  13.6 0.7 compare_and_fusion
  14.3 0.1 copy.20
  14.3 0.1 reshape.76
  14.4 0.1 copy.19
  14.5 0.7 iota_compare_fusion
  15.2 42.1 %collective-permute-done = bf16[2,2048,128]{2,1,0:T(8,128)(2,1)S(1)} collective-permute-done((bf16[2,2048,128]{2,1,0:T(8,128)(2,1)}, bf16[2,2048,128]{2,1,0:T(8,128)(2,1)S(1)}, u32[]{:S(2)}, u32[]{:S(2)}) %collective-permute-start) | collective-permute-done | bytes 1048608 | tf_op jit(solution)/shard_map/ppermute | solution.py:12
  57.4 0.0 copy-start
  57.4 1.0 copy-done
  58.4 0.0 collective-permute-done.1
  58.4 2.0 %pad_maximum_fusion = bf16[2,6144,128]{2,1,0:T(8,128)(2,1)S(1)} fusion(bf16[2,2048,128]{2,1,0:T(8,128)(2,1)} %collective-permute-done.1, bf16[2,2048,128]{2,1,0:T(8,128)(2,1)} %param.5, bf16[2,2048,128]{2,1,0:T(8,128)(2,1)} %copy-done), kind=kLoop, calls=%fused_computation.16 | loop fusion | flops 9437184 | bytes 6291456 | tf_op jit(solution)/shard_map/concatenate | solution.py:16
  60.3 6.6 %gather_fusion = bf16[128,2,128,128]{3,2,1,0:T(8,128)(2,1)} fusion(bf16[2,48,128,128]{3,2,1,0:T(8,128)(2,1)S(1)} %bitcast.114, s32[1024]{0:T(1024)S(1)} %pad_clamp_fusion), kind=kCustom, calls=%fused_computation | custom fusion | bytes 16777728 | tf_op jit(solution)/shard_map/jit(_take)/gather | solution.py:46
  66.9 0.0 slice-start
  66.9 10.5 %copy.21 = bf16[2,128,128,128]{3,2,1,0:T(8,128)(2,1)} copy(bf16[2,128,128,128]{3,2,0,1:T(8,128)(2,1)} %bitcast.116) | data formatting | bytes 16777216 | tf_op jit(solution)/shard_map/jit(_take)/gather | solution.py:46
  77.4 0.0 slice-start.1
  77.4 5.0 %select_select_fusion = bf16[2,16,8,128,128]{4,3,2,1,0:T(8,128)(2,1)S(1)} fusion(bf16[2,16,8,128,128]{4,3,2,1,0:T(8,128)(2,1)} %bitcast.115, pred[16,8]{1,0:T(8,128)(4,1)S(1)} %copy.19, pred[16,8]{1,0:T(8,128)(4,1)S(1)} %iota_compare_fusion), kind=kLoop, calls=%fused_computation.1 | loop fusion | flops 8388608 | bytes 16777472 | tf_op jit(solution)/shard_map/jit(_where)/select_n | solution.py:50
  82.4 0.0 slice-done
  82.4 0.0 slice-done.1
  82.4 0.0 slice-start.2
  82.4 1.2 fusion.19
  83.7 0.0 slice-start.3
  83.7 1.2 fusion.16
  84.9 0.0 slice-done.2
  84.9 1.1 slice-done.3
  86.1 1.3 fusion.37
  87.4 1.3 fusion.34
  88.6 0.0 all-gather.2.cloned.1.call-done
  88.6 2.1 %fusion.13 = f32[128,512]{1,0:T(8,128)S(1)} fusion(bf16[2048,128]{1,0:T(8,128)(2,1)S(1)} %bitcast.117, bf16[2,2048,512]{2,1,0:T(8,128)(2,1)} %all-gather.2.cloned.1.call-done), kind=kOutput, calls=%fused_computation.20 | convolution fusion | flops 268435456 | bytes 2883584 | tf_op jit(solution)/shard_map/dot_general | solution.py:21
  90.7 2.1 %fusion.41 = f32[512,128]{0,1:T(8,128)S(1)} fusion(f32[128,512]{1,0:T(8,128)S(1)} %fusion.13, bf16[2048,128]{1,0:T(8,128)(2,1)S(1)} %bitcast.119, bf16[2,2048,512]{2,1,0:T(8,128)(2,1)} %all-gather.2.cloned.1.call-done), kind=kOutput, calls=%fused_computation.32 | convolution fusion | flops 268500992 | bytes 3145728 | tf_op jit(solution)/shard_map/dot_general | solution.py:21
  92.8 0.1 stack.12
  92.9 0.2 copy.24
  93.0 0.0 copy-start.1
  93.1 2.1 %fusion.12 = f32[128,512]{1,0:T(8,128)S(1)} fusion(bf16[2048,128]{1,0:T(8,128)(2,1)S(1)} %bitcast.120, bf16[2,2048,512]{2,1,0:T(8,128)(2,1)} %all-gather.2.cloned.1.call-done), kind=kOutput, calls=%fused_computation.19 | convolution fusion | flops 268435456 | bytes 2883584 | tf_op jit(solution)/shard_map/dot_general | solution.py:21
  95.1 2.1 %fusion.43 = f32[512,128]{0,1:T(8,128)S(1)} fusion(f32[128,512]{1,0:T(8,128)S(1)} %fusion.12, bf16[2048,128]{1,0:T(8,128)(2,1)S(1)} %bitcast.118, bf16[2,2048,512]{2,1,0:T(8,128)(2,1)} %all-gather.2.cloned.1.call-done), kind=kOutput, calls=%fused_computation.34 | convolution fusion | flops 268500992 | bytes 3145728 | tf_op jit(solution)/shard_map/dot_general | solution.py:21
  97.2 0.1 stack.13
  97.3 0.2 copy.25
  97.5 0.9 pad_maximum_fusion.1
  98.4 0.0 all-reduce.3.cloned.1.call-update
  98.4 0.0 copy-done.1
  98.4 0.6 dynamic-slice
  99.7 72.4 %all-reduce.3.cloned.1.call-done = f32[4,128,2,128]{3,0,2,1:T(4,128)} async-done(((f32[4,128,2,128]{3,0,2,1:T(4,128)}), f32[4,128,2,128]{3,0,2,1:T(4,128)}) %all-reduce.3.cloned.1.call-update) | async-done | bytes 524304
  172.0 0.8 constant_dynamic-slice_fusion
  172.9 5.8 %all_gather.7 = f32[4,16,2,512]{3,0,2,1:T(4,128)S(1)} all-gather(f32[4,16,2,128]{3,0,2,1:T(4,128)S(1)} %constant_dynamic-slice_fusion), channel_id=1, replica_groups=mesh['rows'=8,'cols'=4] {'cols'}, dimensions={3}, use_global_device_ids=true | all-gather | bytes 327680 | tf_op jit(solution)/shard_map/all_gather | solution.py:60
  178.7 0.8 copy.26
  (4 shorter events, 0.0 us)
Async XLA Ops:
  6.5 82.1 %all-gather.2.cloned.1.call-start = ((), (), s32[]{:S(2)}) async-start(), calls=%async_computation | async-start | bytes 5242880 | tf_op jit(solution)/shard_map/all_gather | solution.py:57
  7.3 164.8 %all-reduce.3.cloned.1.call-start = ((), (), s32[]{:S(2)}) async-start(), calls=%async_computation.1 | async-start | bytes 1048576
  7.3 50.1 %collective-permute-start = (bf16[2,2048,128]{2,1,0:T(8,128)(2,1)}, bf16[2,2048,128]{2,1,0:T(8,128)(2,1)S(1)}, u32[]{:S(2)}, u32[]{:S(2)}) collective-permute-start(bf16[2,2048,128]{2,1,0:T(8,128)(2,1)} %param.5), channel_id=1, source_target_pairs={{0,4},{4,8},{8,12},{12,16},{16,20},{20,24},{24,28},{1,5},{5,9},{9,... | collective-permute-start | bytes 3145736 | tf_op jit(solution)/shard_map/ppermute | solution.py:12
  12.2 46.1 %collective-permute-start.1 = (bf16[2,2048,128]{2,1,0:T(8,128)(2,1)}, bf16[2,2048,128]{2,1,0:T(8,128)(2,1)}, u32[]{:S(2)}, u32[]{:S(2)}) collective-permute-start(bf16[2,2048,128]{2,1,0:T(8,128)(2,1)} %param.5), channel_id=1, source_target_pairs={{4,0},{8,4},{12,8},{16,12},{20,16},{24,20},{28,24},{5,1},{9,5},{13... | collective-permute-start | bytes 3145736 | tf_op jit(solution)/shard_map/ppermute | solution.py:15
  57.4 1.0 copy-start
  66.9 15.5 %slice-start = ((s8[8388608]{0:T(1024)(128)(4,1)}), s8[4194304]{0:T(1024)(128)(4,1)S(1)}, s32[]{:S(2)}) async-start(s8[8388608]{0:T(1024)(128)(4,1)} %bitcast.121), calls=%async_computation.2 | async-start | bytes 8388608
  77.4 5.0 %slice-start.1 = ((s8[8388608]{0:T(1024)(128)(4,1)}), s8[4194304]{0:T(1024)(128)(4,1)S(1)}, s32[]{:S(2)}) async-start(s8[8388608]{0:T(1024)(128)(4,1)} %bitcast.121), calls=%async_computation.3 | async-start | bytes 8388608
  82.4 2.5 %slice-start.2 = ((s8[8388608]{0:T(1024)(128)(4,1)}), s8[4194304]{0:T(1024)(128)(4,1)S(1)}, s32[]{:S(2)}) async-start(s8[8388608]{0:T(1024)(128)(4,1)} %bitcast.123), calls=%async_computation.4 | async-start | bytes 8388608
  83.7 2.4 %slice-start.3 = ((s8[8388608]{0:T(1024)(128)(4,1)}), s8[4194304]{0:T(1024)(128)(4,1)S(1)}, s32[]{:S(2)}) async-start(s8[8388608]{0:T(1024)(128)(4,1)} %bitcast.123), calls=%async_computation.5 | async-start | bytes 8388608
  93.0 5.4 %copy-start.1 = (u32[32]{0:T(128)S(1)}, u32[32]{0:T(128)}, u32[]{:S(2)}) copy-start(u32[32]{0:T(128)} %constant.31) | copy-start | bytes 388
Sparse Core Ops, SparseCore 0:
  8.9 37.7 all-gather.1
  98.5 73.4 all-reduce.2
where the time goes:
time: 187 us; the launch traced here: 186 us
  waiting for transfers between devices  115 us (61%)
  local copies, waits for them, and re-layouts  22.3 us (12%)
  between operations  14.2 us (8%)
  matrix products  13.3 us (7%)
  other arithmetic  9.27 us (5%)
  starting transfers between devices  6.27 us (3%)
  blocking collectives  5.79 us (3%)
    unnamed x3, waiting for transfers between devices  73.1 us
    ppermute x1, waiting for transfers between devices, padded(): lax.ppermute(lax.slice_in_dim(block, block.shape[dim] - width, None, axis...  42.1 us
    gather x2, local copies, waits for them, and re-layouts, local(): jnp.take(stacked, local_cols.reshape(-1), axis=1)  17.1 us
    dot_general x4, matrix products, inner_rows(): lax.dot_general(first, second, (((0,), (0,)), ((), ())), preferred_elemen...  8.26 us
    all_gather x1, blocking collectives, local(): return lax.all_gather(shares, 'cols', axis=3, tiled=True)  5.79 us
    dot_general x4, matrix products, apply_blocks(): jnp.einsum('ijpq,ijqk->ipk', mats, vecs, preferred_element_type=jnp.float32)  5 us
    select_n x1, other arithmetic, local(): jnp.where(valid[None, :, :, None, None], picked, jnp.zeros_like(picked))  4.96 us
    ppermute x1, starting transfers between devices, padded(): lax.ppermute(lax.slice_in_dim(block, block.shape[dim] - width, None, axis...  4.94 us
  transfers between devices with their start and end apart: 4, of which 2 were waited for; matrix products, arithmetic and copies ran while one was open for 17% of the time, Pallas kernels for 0%

commit v1 on v0

v1 whole, which is shorter than its diff:
```python
import functools

import jax
import jax.numpy as jnp
from jax import lax
from jax.experimental import pallas as pl
from jax.experimental.pallas import tpu as pltpu
from jax.sharding import PartitionSpec as P

MESH = pl.DeviceIdType.MESH
CHUNKS = 8


def remote(src, dst, send_sem, recv_sem, **device):
    return pltpu.make_async_remote_copy(
        src_ref=src,
        dst_ref=dst,
        send_sem=send_sem,
        recv_sem=recv_sem,
        device_id=device,
        device_id_type=MESH,
    )


def kernel(
    n, groups, reduce_inside,
    cols_ref, counts_ref, right_ref, left_ref, dip_ref, out_ref,
    vecs, left_own, left_all, dip, image, part, landed, final,
    near_send, near_recv, far_send, far_recv, across_send, across_recv,
    mate_send, mate_recv, pass_send, pass_recv,
    local_sem, left_sem, share_send, share_recv, final_send, final_recv,
):
    me = lax.axis_index("rows")
    col = lax.axis_index("cols")
    blocks = right_ref.shape[1]
    slots = dip_ref.shape[1]
    size = right_ref.shape[2]
    width = right_ref.shape[3]
    span = blocks * size
    step_blocks = blocks // CHUNKS
    step_rows = span // CHUNKS

    parity = lax.rem(me, 2)
    partner = me + 1 - 2 * parity
    ahead = me + 2 - 4 * parity
    behind = me - 2 + 4 * parity
    near_off = 2 * blocks * (1 - parity)
    far_off = 2 * blocks * parity
    has_ahead = jnp.logical_and(ahead >= 0, ahead < n)
    has_behind = jnp.logical_and(behind >= 0, behind < n)
    mate = col + 1 - 2 * lax.rem(col, 2)
    across = lax.rem(col + 2, groups)

    own_left = pltpu.make_async_copy(left_ref, left_own, left_sem)
    own_left.start()

    barrier = pltpu.get_barrier_semaphore()
    if reduce_inside:
        for d in range(1, n):
            pl.semaphore_signal(barrier, inc=1, device_id={"rows": lax.rem(me + d, n)}, device_id_type=MESH)
        for d in range(1, groups):
            pl.semaphore_signal(barrier, inc=1, device_id={"cols": lax.rem(col + d, groups)}, device_id_type=MESH)
        pl.semaphore_wait(barrier, n - 1 + groups - 1)
    else:
        pl.semaphore_signal(barrier, inc=1, device_id={"rows": partner}, device_id_type=MESH)
        pl.semaphore_signal(barrier, inc=1, device_id={"cols": mate}, device_id_type=MESH)
        pl.semaphore_signal(barrier, inc=1, device_id={"cols": across}, device_id_type=MESH)

        @pl.when(has_ahead)
        def _():
            pl.semaphore_signal(barrier, inc=1, device_id={"rows": ahead}, device_id_type=MESH)

        @pl.when(has_behind)
        def _():
            pl.semaphore_signal(barrier, inc=1, device_id={"rows": behind}, device_id_type=MESH)

        pl.semaphore_wait(barrier, 3 + has_ahead.astype(jnp.int32) + has_behind.astype(jnp.int32))

    def near(k):
        return remote(
            right_ref.at[:, pl.ds(k * step_blocks, step_blocks)],
            vecs.at[:, pl.ds(far_off + k * step_blocks, step_blocks)],
            near_send.at[k], near_recv.at[k], rows=partner,
        )

    def far(k):
        return remote(
            vecs.at[:, pl.ds(near_off + k * step_blocks, step_blocks)],
            vecs.at[:, pl.ds(far_off + k * step_blocks, step_blocks)],
            far_send.at[k], far_recv.at[k], rows=ahead,
        )

    def to_across(k):
        return remote(left_all.at[col, k], left_all.at[col, k], across_send.at[k], across_recv.at[k], cols=across)

    def to_mate(k):
        return remote(left_all.at[col, k], left_all.at[col, k], mate_send.at[k], mate_recv.at[k], cols=mate)

    def passed(k):
        return remote(left_all.at[across, k], left_all.at[across, k], pass_send.at[k], pass_recv.at[k], cols=mate)

    for k in range(CHUNKS):
        near(k).start()
    own_left.wait()
    for k in range(CHUNKS):
        for c in range(2):
            left_all[col, k, c * width:(c + 1) * width, :] = left_own[c, k * step_rows:(k + 1) * step_rows, :].T
        to_across(k).start()
        to_mate(k).start()
    own_vecs = pltpu.make_async_copy(right_ref, vecs.at[:, pl.ds(blocks, blocks)], local_sem.at[0])
    own_vecs.start()
    own_dip = pltpu.make_async_copy(dip_ref, dip, local_sem.at[1])
    own_dip.start()
    for k in range(CHUNKS):
        near(k).wait_recv()

        @pl.when(has_ahead)
        def _():
            far(k).start()

        to_across(k).wait_recv()
        passed(k).start()
    own_vecs.wait()
    own_dip.wait()
    for k in range(CHUNKS):

        @pl.when(has_behind)
        def _():
            far(k).wait_recv()

    first = (me - 1) * blocks

    def block_row(i, carry):
        count = counts_ref[i]
        total = jnp.zeros((size, 2 * width), jnp.float32)
        for j in range(slots):
            at = jnp.clip(cols_ref[i, j] - first, 0, 3 * blocks - 1)
            real = vecs[0, at]
            imag = vecs[1, at]
            rhs = jnp.concatenate(
                [jnp.concatenate([real, imag], axis=1), jnp.concatenate([-imag, real], axis=1)], axis=0
            )
            lhs = jnp.concatenate([dip[i, j, 0], dip[i, j, 1]], axis=1)
            lhs = jnp.where(j < count, lhs, jnp.zeros_like(lhs))
            total = total + jnp.dot(lhs, rhs, preferred_element_type=jnp.float32)
        image[pl.ds(i * size, size), :] = total.astype(image.dtype)
        return carry

    lax.fori_loop(0, blocks, block_row, 0)

    for k in range(CHUNKS):
        to_mate(k).wait_recv()
        passed(k).wait_recv()

    def product(g):
        total = jnp.zeros((2 * width, 2 * width), jnp.float32)
        for k in range(CHUNKS):
            total = total + jnp.dot(
                left_all[g, k], image[k * step_rows:(k + 1) * step_rows, :], preferred_element_type=jnp.float32
            )
        real_part = total[:width, :width] + total[width:, width:]
        imag_part = total[:width, width:] - total[width:, :width]
        return real_part, imag_part

    if not reduce_inside:
        for g in range(groups):
            real_part, imag_part = product(g)
            out_ref[g, 0] = real_part
            out_ref[g, 1] = imag_part
    else:
        share = width // n
        for g in range(groups):
            real_part, imag_part = product(g)
            part[:, g, 0] = real_part.astype(part.dtype).reshape(n, share, width)
            part[:, g, 1] = imag_part.astype(part.dtype).reshape(n, share, width)

        def give(d):
            peer = lax.rem(me + d, n)
            return remote(part.at[peer], landed.at[me], share_send.at[peer], share_recv.at[me], rows=peer)

        def take(d):
            peer = lax.rem(me + d, n)
            return remote(part.at[peer], landed.at[peer], share_send.at[peer], share_recv.at[peer], rows=peer)

        for d in range(1, n):
            give(d).start()
        total = part[me].astype(jnp.float32)
        for d in range(1, n):
            take(d).wait_recv()
            total = total + landed[lax.rem(me + d, n)].astype(jnp.float32)
        final[col] = total

        def spread(d):
            peer = lax.rem(col + d, groups)
            return remote(final.at[col], final.at[col], final_send.at[d], final_recv.at[col], cols=peer)

        def gather(d):
            peer = lax.rem(col + d, groups)
            return remote(final.at[peer], final.at[peer], final_send.at[d], final_recv.at[peer], cols=peer)

        for d in range(1, groups):
            spread(d).start()
        for d in range(1, groups):
            gather(d).wait_recv()
        for c in range(groups):
            out_ref[:, :, :, c * width:(c + 1) * width] = final[c]
        for d in range(1, n):
            give(d).wait_send()
        for d in range(1, groups):
            spread(d).wait_send()

    for k in range(CHUNKS):
        near(k).wait_send()

        @pl.when(has_ahead)
        def _():
            far(k).wait_send()

        to_across(k).wait_send()
        to_mate(k).wait_send()
        passed(k).wait_send()


def local(n, groups, right_vecs, left_vecs, dip_blocks, block_cols, block_counts):
    span, width = right_vecs.shape[1:]
    blocks, slots, _, size, _ = dip_blocks.shape
    share = width // n
    reduce_inside = share % 16 == 0
    right = right_vecs.reshape(2, blocks, size, width)
    if reduce_inside:
        out_shape = (groups, 2, share, groups * width)
        part_shape = (n, groups, 2, share, width)
        final_shape = (groups, groups, 2, share, width)
    else:
        out_shape = (groups, 2, width, width)
        part_shape = final_shape = (1, 1, 1, 16, 128)
    dma = pltpu.SemaphoreType.DMA
    result = pl.pallas_call(
        functools.partial(kernel, n, groups, reduce_inside),
        out_shape=jax.ShapeDtypeStruct(out_shape, jnp.float32),
        in_specs=[pl.BlockSpec(memory_space=pltpu.SMEM)] * 2 + [pl.BlockSpec(memory_space=pl.ANY)] * 3,
        out_specs=pl.BlockSpec(memory_space=pltpu.VMEM),
        scratch_shapes=[
            pltpu.VMEM((2, 3 * blocks, size, width), jnp.bfloat16),
            pltpu.VMEM((2, span, width), jnp.bfloat16),
            pltpu.VMEM((groups, CHUNKS, 2 * width, span // CHUNKS), jnp.bfloat16),
            pltpu.VMEM(dip_blocks.shape, jnp.bfloat16),
            pltpu.VMEM((span, 2 * width), jnp.bfloat16),
            pltpu.VMEM(part_shape, jnp.bfloat16),
            pltpu.VMEM(part_shape, jnp.bfloat16),
            pltpu.VMEM(final_shape, jnp.float32),
        ] + [dma((CHUNKS,))] * 10 + [
            dma((2,)), dma, dma((n,)), dma((n,)), dma((groups,)), dma((groups,)),
        ],
        compiler_params=pltpu.CompilerParams(
            collective_id=0, has_side_effects=True, vmem_limit_bytes=40 * 1024 * 1024
        ),
    )(block_cols, block_counts, right, left_vecs, dip_blocks)
    if reduce_inside:
        return jnp.transpose(result, (0, 2, 1, 3))
    shares = lax.psum_scatter(jnp.transpose(result, (0, 2, 1, 3)), "rows", scatter_dimension=1, tiled=True)
    return lax.all_gather(shares, "cols", axis=3, tiled=True)


def solution(mesh):
    in_specs = (
        P(None, "rows", "cols"),
        P(None, "rows", "cols"),
        P("rows", None, None, None, None),
        P("rows", None),
        P("rows"),
    )
    out_specs = P(None, "rows", None, None)
    body = functools.partial(local, mesh.shape["rows"], mesh.shape["cols"])
    return jax.shard_map(body, mesh=mesh, in_specs=in_specs, out_specs=out_specs, check_vma=False)
```

time: 187 us -> 59.6 us (0.32)
  waiting for transfers between devices: 115 us -> 0 us
  Pallas kernels: 0 us -> 51.1 us
  between operations: 14.2 us -> 0.01 us
  local copies, waits for them, and re-layouts: 22.3 us -> 8.15 us
  matrix products: 13.3 us -> 0 us
  other arithmetic: 9.27 us -> 0 us
  starting transfers between devices: 6.27 us -> 0 us
  blocking collectives: 5.79 us -> 0 us
    unnamed x3 -> x0, waiting for transfers between devices: 73.1 us -> none
    pallas_call x0 -> x1, Pallas kernels: none -> 51.1 us  [local(): pl.pallas_call(functools.partial(kernel, n, groups, reduce_inside), out_s...]
    ppermute x2 -> x0, waiting for transfers between devices: 42.1 us -> none  [the longest x1 42.1 us: padded(): lax.ppermute(lax.slice_in_dim(block, block.shape[dim] - width, None, axis...]
    gather x2 -> x0, local copies, waits for them, and re-layouts: 17.1 us -> none  [local(): jnp.take(stacked, local_cols.reshape(-1), axis=1)]
    dot_general x8 -> x0, matrix products: 13.3 us -> none  [the longest x4 8.26 us: inner_rows(): lax.dot_general(first, second, (((0,), (0,)), ((), ())), preferred_elemen...]
    ppermute x2 -> x0, starting transfers between devices: 6.23 us -> none  [the longest x1 4.94 us: padded(): lax.ppermute(lax.slice_in_dim(block, block.shape[dim] - width, None, axis...]
    all_gather x1 -> x0, blocking collectives: 5.79 us -> none  [local(): return lax.all_gather(shares, 'cols', axis=3, tiled=True)]
    select_n x2 -> x0, other arithmetic: 4.96 us -> none  [the longest x1 4.96 us: local(): jnp.where(valid[None, :, :, None, None], picked, jnp.zeros_like(picked))]
  transfers between devices with their start and end apart: 4 -> 0, of which waited for: 2 -> 0; matrix products, arithmetic and copies ran while one was open for 17% -> 0% of each run, Pallas kernels for 0% -> 0%
where the time goes in v1:
time: 59.6 us; the launch traced here: 59.2 us
  Pallas kernels  51.1 us (86%)
  local copies, waits for them, and re-layouts  8.15 us (14%)
    pallas_call x1, Pallas kernels, local(): pl.pallas_call(functools.partial(kernel, n, groups, reduce_inside), out_s...  51.1 us
    unnamed x9, local copies, waits for them, and re-layouts  7.24 us

profile of v1, /device:TPU:0, one launch (start us, length us, event | category | flops | bytes accessed | tf_op | source)
XLA Modules:
  0.0 59.2 jit_solution(23891015693281624)
XLA Ops:
  0.0 0.8 %copy.6.cols_ref = s32[16,8]{1,0:T(8,128)S(1)} copy(s32[16,8]{0,1:T(8,128)} %param.8) | data formatting | bytes 1024 | tf_op args[3]
  0.8 0.0 copy-start
  0.8 3.4 %copy-done = bf16[16,8,2,128,128]{4,3,2,1,0:T(8,128)(2,1)S(1)} copy-done((bf16[16,8,2,128,128]{4,3,2,1,0:T(8,128)(2,1)S(1)}, bf16[16,8,2,128,128]{4,3,2,1,0:T(8,128)(2,1)}, u32[]{:S(2)}) %copy-start) | copy-done | bytes 8388632
  4.1 0.0 copy-start.1
  4.1 1.2 %copy-done.1 = bf16[2,2048,128]{2,1,0:T(8,128)(2,1)S(1)} copy-done((bf16[2,2048,128]{2,1,0:T(8,128)(2,1)S(1)}, bf16[2,2048,128]{2,1,0:T(8,128)(2,1)}, u32[]{:S(2)}) %copy-start.1) | copy-done | bytes 1048600
  5.4 0.0 copy-start.2
  5.4 1.2 %copy-done.2 = bf16[2,2048,128]{2,1,0:T(8,128)(2,1)S(1)} copy-done((bf16[2,2048,128]{2,1,0:T(8,128)(2,1)S(1)}, bf16[2,2048,128]{2,1,0:T(8,128)(2,1)}, u32[]{:S(2)}) %copy-start.2) | copy-done | bytes 1048600
  6.6 0.0 copy-start.3
  6.6 0.7 %copy-done.3 = s32[16]{0:T(128)S(1)} copy-done((s32[16]{0:T(128)S(1)}, s32[16]{0:T(128)}, u32[]{:S(2)}) %copy-start.3) | copy-done | bytes 88
  7.2 51.1 %shard_map.55 = f32[4,2,16,512]{3,2,1,0:T(8,128)S(1)} custom-call(s32[16,8]{1,0:T(8,128)S(1)} %copy.6.cols_ref, s32[16]{0:T(128)S(1)} %copy-done.3, bf16[2,16,128,128]{3,2,1,0:T(8,128)(2,1)S(1)} %bitcast.2, bf16[2,2048,128]{2,1,0:T(8,128)(2,1)S(1)} %copy-done.2, bf16[16,8,2,128,128]{4,3,2,1,0:T(8,128)(2,1)S(1)} %copy-done), custom_call_target="tpu_custom_call" | custom-call | tf_op jit(solution)/shard_map/pallas_call | solution.py:238
  58.3 0.9 %copy.7 = f32[4,16,2,512]{3,2,1,0:T(2,128)} copy(f32[4,16,2,512]{3,1,2,0:T(8,128)S(1)} %bitcast.3) | data formatting | bytes 524288 | tf_op jit(solution)/shard_map/transpose | solution.py:260
Async XLA Ops:
  0.8 3.4 %copy-start = (bf16[16,8,2,128,128]{4,3,2,1,0:T(8,128)(2,1)S(1)}, bf16[16,8,2,128,128]{4,3,2,1,0:T(8,128)(2,1)}, u32[]{:S(2)}) copy-start(bf16[16,8,2,128,128]{4,3,2,1,0:T(8,128)(2,1)} %dip_ref.1) | copy-start | bytes 25165828
  4.1 1.2 %copy-start.1 = (bf16[2,2048,128]{2,1,0:T(8,128)(2,1)S(1)}, bf16[2,2048,128]{2,1,0:T(8,128)(2,1)}, u32[]{:S(2)}) copy-start(bf16[2,2048,128]{2,1,0:T(8,128)(2,1)} %param.5) | copy-start | bytes 3145732
  5.4 1.2 %copy-start.2 = (bf16[2,2048,128]{2,1,0:T(8,128)(2,1)S(1)}, bf16[2,2048,128]{2,1,0:T(8,128)(2,1)}, u32[]{:S(2)}) copy-start(bf16[2,2048,128]{2,1,0:T(8,128)(2,1)} %left_ref.1) | copy-start | bytes 3145732
  6.6 0.7 %copy-start.3 = (s32[16]{0:T(128)S(1)}, s32[16]{0:T(128)}, u32[]{:S(2)}) copy-start(s32[16]{0:T(128)} %counts_ref.1) | copy-start | bytes 196

commit v2 on v1

--- a/solution.py
+++ b/solution.py
@@ -8,7 +8,9 @@
 from jax.sharding import PartitionSpec as P
 
 MESH = pl.DeviceIdType.MESH
-CHUNKS = 8
+CHUNKS = 16
+LEFT_CHUNKS = 8
+HALVES = 2
 
 
 def remote(src, dst, send_sem, recv_sem, **device):
@@ -25,7 +27,7 @@
 def kernel(
     n, groups, reduce_inside,
     cols_ref, counts_ref, right_ref, left_ref, dip_ref, out_ref,
-    vecs, left_own, left_all, dip, image, part, landed, final,
+    vecs, left_own, left_all, dip, pairs, mats, image, part, landed, final,
     near_send, near_recv, far_send, far_recv, across_send, across_recv,
     mate_send, mate_recv, pass_send, pass_recv,
     local_sem, left_sem, share_send, share_recv, final_send, final_recv,
@@ -38,7 +40,7 @@
     width = right_ref.shape[3]
     span = blocks * size
     step_blocks = blocks // CHUNKS
-    step_rows = span // CHUNKS
+    step_rows = span // LEFT_CHUNKS
 
     parity = lax.rem(me, 2)
     partner = me + 1 - 2 * parity
@@ -53,6 +55,8 @@
 
     own_left = pltpu.make_async_copy(left_ref, left_own, left_sem)
     own_left.start()
+    own_vecs = pltpu.make_async_copy(right_ref, vecs.at[:, pl.ds(blocks, blocks)], local_sem.at[0])
+    own_dip = pltpu.make_async_copy(dip_ref, dip, local_sem.at[1])
 
     barrier = pltpu.get_barrier_semaphore()
     if reduce_inside:
@@ -102,15 +106,43 @@
     for k in range(CHUNKS):
         near(k).start()
     own_left.wait()
-    for k in range(CHUNKS):
+    for k in range(LEFT_CHUNKS):
         for c in range(2):
             left_all[col, k, c * width:(c + 1) * width, :] = left_own[c, k * step_rows:(k + 1) * step_rows, :].T
         to_across(k).start()
         to_mate(k).start()
-    own_vecs = pltpu.make_async_copy(right_ref, vecs.at[:, pl.ds(blocks, blocks)], local_sem.at[0])
     own_vecs.start()
-    own_dip = pltpu.make_async_copy(dip_ref, dip, local_sem.at[1])
     own_dip.start()
+
+    def pair(at):
+        real = vecs[0, at]
+        imag = vecs[1, at]
+        pairs[at, :size, :width] = real
+        pairs[at, :size, width:] = imag
+        pairs[at, size:, :width] = -imag
+        pairs[at, size:, width:] = real
+
+    def lay_out(i, carry):
+        count = counts_ref[i]
+        for j in range(slots):
+            for c in range(2):
+                block = dip[i, j, c]
+                at = (2 * j + c) * size
+                mats[i, :, at:at + size] = jnp.where(j < count, block, jnp.zeros_like(block))
+        return carry
+
+    def far_pairs(k):
+        @pl.when(has_behind)
+        def _():
+            far(k).wait_recv()
+
+        for b in range(step_blocks):
+            pair(far_off + k * step_blocks + b)
+
+    lag = 2
+    half_way = CHUNKS // 2
+    every = CHUNKS // LEFT_CHUNKS
+    per_step = blocks // half_way
     for k in range(CHUNKS):
         near(k).wait_recv()
 
@@ -118,43 +150,46 @@
         def _():
             far(k).start()
 
-        to_across(k).wait_recv()
-        passed(k).start()
-    own_vecs.wait()
-    own_dip.wait()
-    for k in range(CHUNKS):
-
-        @pl.when(has_behind)
-        def _():
-            far(k).wait_recv()
+        if k % every == every - 1:
+            to_across(k // every).wait_recv()
+            passed(k // every).start()
+        for b in range(step_blocks):
+            pair(near_off + k * step_blocks + b)
+        if k < half_way:
+            if k == 0:
+                own_vecs.wait()
+            for b in range(per_step):
+                pair(blocks + k * per_step + b)
+        else:
+            if k == half_way:
+                own_dip.wait()
+            start = (k - half_way) * per_step
+            lax.fori_loop(start, start + per_step, lay_out, 0)
+        if k >= lag:
+            far_pairs(k - lag)
+    for k in range(CHUNKS - lag, CHUNKS):
+        far_pairs(k)
 
     first = (me - 1) * blocks
 
     def block_row(i, carry):
-        count = counts_ref[i]
         total = jnp.zeros((size, 2 * width), jnp.float32)
         for j in range(slots):
-            at = jnp.clip(cols_ref[i, j] - first, 0, 3 * blocks - 1)
-            real = vecs[0, at]
-            imag = vecs[1, at]
-            rhs = jnp.concatenate(
-                [jnp.concatenate([real, imag], axis=1), jnp.concatenate([-imag, real], axis=1)], axis=0
-            )
-            lhs = jnp.concatenate([dip[i, j, 0], dip[i, j, 1]], axis=1)
-            lhs = jnp.where(j < count, lhs, jnp.zeros_like(lhs))
-            total = total + jnp.dot(lhs, rhs, preferred_element_type=jnp.float32)
+            at = jnp.clip(cols_ref[j, i] - first, 0, 3 * blocks - 1)
+            lhs = mats[i, :, 2 * j * size:2 * (j + 1) * size]
+            total = total + jnp.dot(lhs, pairs[at], preferred_element_type=jnp.float32)
         image[pl.ds(i * size, size), :] = total.astype(image.dtype)
         return carry
 
     lax.fori_loop(0, blocks, block_row, 0)
 
-    for k in range(CHUNKS):
+    for k in range(LEFT_CHUNKS):
         to_mate(k).wait_recv()
         passed(k).wait_recv()
 
     def product(g):
         total = jnp.zeros((2 * width, 2 * width), jnp.float32)
-        for k in range(CHUNKS):
+        for k in range(LEFT_CHUNKS):
             total = total + jnp.dot(
                 left_all[g, k], image[k * step_rows:(k + 1) * step_rows, :], preferred_element_type=jnp.float32
             )
@@ -169,45 +204,51 @@
             out_ref[g, 1] = imag_part
     else:
         share = width // n
-        for g in range(groups):
-            real_part, imag_part = product(g)
-            part[:, g, 0] = real_part.astype(part.dtype).reshape(n, share, width)
-            part[:, g, 1] = imag_part.astype(part.dtype).reshape(n, share, width)
-
-        def give(d):
+        half = groups // HALVES
+        order = sorted(range(1, n), key=lambda d: abs(d - n // 2))
+
+        def give(h, d):
             peer = lax.rem(me + d, n)
-            return remote(part.at[peer], landed.at[me], share_send.at[peer], share_recv.at[me], rows=peer)
-
-        def take(d):
+            return remote(part.at[h, peer], landed.at[h, me], share_send.at[h, peer], share_recv.at[h, me], rows=peer)
+
+        def take(h, d):
             peer = lax.rem(me + d, n)
-            return remote(part.at[peer], landed.at[peer], share_send.at[peer], share_recv.at[peer], rows=peer)
-
-        for d in range(1, n):
-            give(d).start()
-        total = part[me].astype(jnp.float32)
-        for d in range(1, n):
-            take(d).wait_recv()
-            total = total + landed[lax.rem(me + d, n)].astype(jnp.float32)
-        final[col] = total
-
-        def spread(d):
+            return remote(part.at[h, peer], landed.at[h, peer], share_send.at[h, peer], share_recv.at[h, peer], rows=peer)
+
+        def spread(h, d):
             peer = lax.rem(col + d, groups)
-            return remote(final.at[col], final.at[col], final_send.at[d], final_recv.at[col], cols=peer)
-
-        def gather(d):
+            return remote(final.at[h, col], final.at[h, col], final_send.at[h, d], final_recv.at[h, col], cols=peer)
+
+        def gather(h, d):
             peer = lax.rem(col + d, groups)
-            return remote(final.at[peer], final.at[peer], final_send.at[d], final_recv.at[peer], cols=peer)
-
-        for d in range(1, groups):
-            spread(d).start()
-        for d in range(1, groups):
-            gather(d).wait_recv()
-        for c in range(groups):
-            out_ref[:, :, :, c * width:(c + 1) * width] = final[c]
-        for d in range(1, n):
-            give(d).wait_send()
-        for d in range(1, groups):
-            spread(d).wait_send()
+            return remote(final.at[h, peer], final.at[h, peer], final_send.at[h, d], final_recv.at[h, peer], cols=peer)
+
+        for h in range(HALVES):
+            for g in range(half):
+                real_part, imag_part = product(h * half + g)
+                part[h, :, g, 0] = real_part.astype(part.dtype).reshape(n, share, width)
+                part[h, :, g, 1] = imag_part.astype(part.dtype).reshape(n, share, width)
+            for d in order:
+                give(h, d).start()
+        for h in range(HALVES):
+            total = part[h, me].astype(jnp.float32)
+            for d in order[::-1]:
+                take(h, d).wait_recv()
+                total = total + landed[h, lax.rem(me + d, n)].astype(jnp.float32)
+            final[h, col] = total
+            for d in (2, 3, 1):
+                spread(h, d).start()
+        for h in range(HALVES):
+            for d in range(1, groups):
+                gather(h, d).wait_recv()
+            for c in range(groups):
+                for part_at in range(2):
+                    out_ref[h * half:(h + 1) * half, :, part_at, c * width:(c + 1) * width] = final[h, c, :, part_at]
+        for h in range(HALVES):
+            for d in order:
+                give(h, d).wait_send()
+            for d in range(1, groups):
+                spread(h, d).wait_send()
 
     for k in range(CHUNKS):
         near(k).wait_send()
@@ -216,6 +257,7 @@
         def _():
             far(k).wait_send()
 
+    for k in range(LEFT_CHUNKS):
         to_across(k).wait_send()
         to_mate(k).wait_send()
         passed(k).wait_send()
@@ -228,9 +270,10 @@
     reduce_inside = share % 16 == 0
     right = right_vecs.reshape(2, blocks, size, width)
     if reduce_inside:
-        out_shape = (groups, 2, share, groups * width)
-        part_shape = (n, groups, 2, share, width)
-        final_shape = (groups, groups, 2, share, width)
+        half = groups // HALVES
+        out_shape = (groups, share, 2, groups * width)
+        part_shape = (HALVES, n, half, 2, share, width)
+        final_shape = (HALVES, groups, half, 2, share, width)
     else:
         out_shape = (groups, 2, width, width)
         part_shape = final_shape = (1, 1, 1, 16, 128)
@@ -243,21 +286,23 @@
         scratch_shapes=[
             pltpu.VMEM((2, 3 * blocks, size, width), jnp.bfloat16),
             pltpu.VMEM((2, span, width), jnp.bfloat16),
-            pltpu.VMEM((groups, CHUNKS, 2 * width, span // CHUNKS), jnp.bfloat16),
+            pltpu.VMEM((groups, LEFT_CHUNKS, 2 * width, span // LEFT_CHUNKS), jnp.bfloat16),
             pltpu.VMEM(dip_blocks.shape, jnp.bfloat16),
+            pltpu.VMEM((3 * blocks, 2 * size, 2 * width), jnp.bfloat16),
+            pltpu.VMEM((blocks, size, 2 * slots * size), jnp.bfloat16),
             pltpu.VMEM((span, 2 * width), jnp.bfloat16),
             pltpu.VMEM(part_shape, jnp.bfloat16),
             pltpu.VMEM(part_shape, jnp.bfloat16),
             pltpu.VMEM(final_shape, jnp.float32),
-        ] + [dma((CHUNKS,))] * 10 + [
-            dma((2,)), dma, dma((n,)), dma((n,)), dma((groups,)), dma((groups,)),
+        ] + [dma((CHUNKS,))] * 4 + [dma((LEFT_CHUNKS,))] * 6 + [
+            dma((2,)), dma, dma((HALVES, n)), dma((HALVES, n)), dma((HALVES, groups)), dma((HALVES, groups)),
         ],
         compiler_params=pltpu.CompilerParams(
-            collective_id=0, has_side_effects=True, vmem_limit_bytes=40 * 1024 * 1024
+            collective_id=0, has_side_effects=True, vmem_limit_bytes=60 * 1024 * 1024
         ),
-    )(block_cols, block_counts, right, left_vecs, dip_blocks)
+    )(block_cols.T, block_counts, right, left_vecs, dip_blocks)
     if reduce_inside:
-        return jnp.transpose(result, (0, 2, 1, 3))
+        return result
     shares = lax.psum_scatter(jnp.transpose(result, (0, 2, 1, 3)), "rows", scatter_dimension=1, tiled=True)
     return lax.all_gather(shares, "cols", axis=3, tiled=True)
 

time: 59.6 us -> 53.1 us (0.89)
  local copies, waits for them, and re-layouts: 8.15 us -> 1.67 us
    unnamed x9 -> x1, local copies, waits for them, and re-layouts: 7.24 us -> 1.67 us
    transpose x1 -> x0, local copies, waits for them, and re-layouts: 0.91 us -> none  [local(): return jnp.transpose(result, (0, 2, 1, 3))]
where the time goes in v2:
time: 53.1 us; the launch traced here: 52.9 us
  Pallas kernels  51.3 us (97%)
  local copies, waits for them, and re-layouts  1.67 us (3%)
    pallas_call x1, Pallas kernels, local(): pl.pallas_call(functools.partial(kernel, n, groups, reduce_inside), out_s...  51.3 us
    unnamed x1, local copies, waits for them, and re-layouts  1.67 us

profile of v2, /device:TPU:0, one launch (start us, length us, event | category | flops | bytes accessed | tf_op | source)
XLA Modules:
  0.0 52.9 jit_solution(17110772984891796527)
XLA Ops:
  0.0 51.3 %shard_map.55 = f32[4,16,2,512]{3,2,1,0:T(2,128)} custom-call(s32[8,16]{1,0:T(8,128)} %bitcast.3, s32[16]{0:T(128)} %counts_ref.1, bf16[2,16,128,128]{3,2,1,0:T(8,128)(2,1)} %bitcast.2, bf16[2,2048,128]{2,1,0:T(8,128)(2,1)} %left_ref.1, bf16[16,8,2,128,128]{4,3,2,1,0:T(8,128)(2,1)} %dip_ref.1), custom_call_target="tpu_custom_call" | custom-call | tf_op jit(solution)/shard_map/pallas_call | solution.py:281
  51.3 1.7 %copy.7 = f32[4,16,2,512]{3,2,1,0:T(2,128)} copy(f32[4,16,2,512]{3,2,1,0:T(2,128)} %shard_map.55) | data formatting | bytes 524288

commit v3 on v2

--- a/solution.py
+++ b/solution.py
@@ -80,17 +80,23 @@
 
         pl.semaphore_wait(barrier, 3 + has_ahead.astype(jnp.int32) + has_behind.astype(jnp.int32))
 
+    def got(k):
+        return step_blocks * (k * parity + (CHUNKS - 1 - k) * (1 - parity))
+
+    def sent(k):
+        return step_blocks * (k * (1 - parity) + (CHUNKS - 1 - k) * parity)
+
     def near(k):
         return remote(
-            right_ref.at[:, pl.ds(k * step_blocks, step_blocks)],
-            vecs.at[:, pl.ds(far_off + k * step_blocks, step_blocks)],
+            right_ref.at[:, pl.ds(sent(k), step_blocks)],
+            vecs.at[:, pl.ds(far_off + sent(k), step_blocks)],
             near_send.at[k], near_recv.at[k], rows=partner,
         )
 
     def far(k):
         return remote(
-            vecs.at[:, pl.ds(near_off + k * step_blocks, step_blocks)],
-            vecs.at[:, pl.ds(far_off + k * step_blocks, step_blocks)],
+            vecs.at[:, pl.ds(near_off + got(k), step_blocks)],
+            vecs.at[:, pl.ds(far_off + got(k), step_blocks)],
             far_send.at[k], far_recv.at[k], rows=ahead,
         )
 
@@ -137,9 +143,9 @@
             far(k).wait_recv()
 
         for b in range(step_blocks):
-            pair(far_off + k * step_blocks + b)
-
-    lag = 2
+            pair(far_off + got(k) + b)
+
+    lag = CHUNKS // 4
     half_way = CHUNKS // 2
     every = CHUNKS // LEFT_CHUNKS
     per_step = blocks // half_way
@@ -154,7 +160,7 @@
             to_across(k // every).wait_recv()
             passed(k // every).start()
         for b in range(step_blocks):
-            pair(near_off + k * step_blocks + b)
+            pair(near_off + got(k) + b)
         if k < half_way:
             if k == 0:
                 own_vecs.wait()
@@ -167,21 +173,23 @@
             lax.fori_loop(start, start + per_step, lay_out, 0)
         if k >= lag:
             far_pairs(k - lag)
+    first = (me - 1) * blocks
+
+    def block_row(at, carry):
+        i = at * parity + (blocks - 1 - at) * (1 - parity)
+        total = jnp.zeros((size, 2 * width), jnp.float32)
+        for j in range(slots):
+            source = jnp.clip(cols_ref[j, i] - first, 0, 3 * blocks - 1)
+            lhs = mats[i, :, 2 * j * size:2 * (j + 1) * size]
+            total = total + jnp.dot(lhs, pairs[source], preferred_element_type=jnp.float32)
+        image[pl.ds(i * size, size), :] = total.astype(image.dtype)
+        return carry
+
+    ready = blocks - lag * step_blocks
+    lax.fori_loop(0, ready, block_row, 0, unroll=4)
     for k in range(CHUNKS - lag, CHUNKS):
         far_pairs(k)
-
-    first = (me - 1) * blocks
-
-    def block_row(i, carry):
-        total = jnp.zeros((size, 2 * width), jnp.float32)
-        for j in range(slots):
-            at = jnp.clip(cols_ref[j, i] - first, 0, 3 * blocks - 1)
-            lhs = mats[i, :, 2 * j * size:2 * (j + 1) * size]
-            total = total + jnp.dot(lhs, pairs[at], preferred_element_type=jnp.float32)
-        image[pl.ds(i * size, size), :] = total.astype(image.dtype)
-        return carry
-
-    lax.fori_loop(0, blocks, block_row, 0)
+    lax.fori_loop(ready, blocks, block_row, 0, unroll=4)
 
     for k in range(LEFT_CHUNKS):
         to_mate(k).wait_recv()

time: 53.1 us -> 49 us (0.923)
  Pallas kernels: 51.3 us -> 47.1 us
    pallas_call x1, Pallas kernels: 51.3 us -> 47.1 us  [local(): pl.pallas_call(functools.partial(kernel, n, groups, reduce_inside), out_s...]
where the time goes in v3:
time: 49 us; the launch traced here: 48.8 us
  Pallas kernels  47.1 us (96%)
  local copies, waits for them, and re-layouts  1.67 us (3%)
    pallas_call x1, Pallas kernels, local(): pl.pallas_call(functools.partial(kernel, n, groups, reduce_inside), out_s...  47.1 us
    unnamed x1, local copies, waits for them, and re-layouts  1.67 us

profile of v3, /device:TPU:0, one launch (start us, length us, event | category | flops | bytes accessed | tf_op | source)
XLA Modules:
  0.0 48.8 jit_solution(199503662116715764)
XLA Ops:
  0.0 47.1 %shard_map.55 = f32[4,16,2,512]{3,2,1,0:T(2,128)} custom-call(s32[8,16]{1,0:T(8,128)} %bitcast.3, s32[16]{0:T(128)} %counts_ref.1, bf16[2,16,128,128]{3,2,1,0:T(8,128)(2,1)} %bitcast.2, bf16[2,2048,128]{2,1,0:T(8,128)(2,1)} %left_ref.1, bf16[16,8,2,128,128]{4,3,2,1,0:T(8,128)(2,1)} %dip_ref.1), custom_call_target="tpu_custom_call" | custom-call | tf_op jit(solution)/shard_map/pallas_call | solution.py:289
  47.2 1.7 %copy.7 = f32[4,16,2,512]{3,2,1,0:T(2,128)} copy(f32[4,16,2,512]{3,2,1,0:T(2,128)} %shard_map.55) | data formatting | bytes 524288

commit v4 on v3

--- a/solution.py
+++ b/solution.py
@@ -30,7 +30,7 @@
     vecs, left_own, left_all, dip, pairs, mats, image, part, landed, final,
     near_send, near_recv, far_send, far_recv, across_send, across_recv,
     mate_send, mate_recv, pass_send, pass_recv,
-    local_sem, left_sem, share_send, share_recv, final_send, final_recv,
+    local_sem, left_sem, share_send, share_recv, final_send, final_recv, round_sem,
 ):
     me = lax.axis_index("rows")
     col = lax.axis_index("cols")
@@ -59,26 +59,22 @@
     own_dip = pltpu.make_async_copy(dip_ref, dip, local_sem.at[1])
 
     barrier = pltpu.get_barrier_semaphore()
-    if reduce_inside:
-        for d in range(1, n):
-            pl.semaphore_signal(barrier, inc=1, device_id={"rows": lax.rem(me + d, n)}, device_id_type=MESH)
-        for d in range(1, groups):
-            pl.semaphore_signal(barrier, inc=1, device_id={"cols": lax.rem(col + d, groups)}, device_id_type=MESH)
-        pl.semaphore_wait(barrier, n - 1 + groups - 1)
-    else:
-        pl.semaphore_signal(barrier, inc=1, device_id={"rows": partner}, device_id_type=MESH)
-        pl.semaphore_signal(barrier, inc=1, device_id={"cols": mate}, device_id_type=MESH)
-        pl.semaphore_signal(barrier, inc=1, device_id={"cols": across}, device_id_type=MESH)
+    def greet(sem):
+        pl.semaphore_signal(sem, inc=1, device_id={"rows": partner}, device_id_type=MESH)
+        pl.semaphore_signal(sem, inc=1, device_id={"cols": mate}, device_id_type=MESH)
+        pl.semaphore_signal(sem, inc=1, device_id={"cols": across}, device_id_type=MESH)
 
         @pl.when(has_ahead)
         def _():
-            pl.semaphore_signal(barrier, inc=1, device_id={"rows": ahead}, device_id_type=MESH)
+            pl.semaphore_signal(sem, inc=1, device_id={"rows": ahead}, device_id_type=MESH)
 
         @pl.when(has_behind)
         def _():
-            pl.semaphore_signal(barrier, inc=1, device_id={"rows": behind}, device_id_type=MESH)
-
-        pl.semaphore_wait(barrier, 3 + has_ahead.astype(jnp.int32) + has_behind.astype(jnp.int32))
+            pl.semaphore_signal(sem, inc=1, device_id={"rows": behind}, device_id_type=MESH)
+
+    neighbours = 3 + has_ahead.astype(jnp.int32) + has_behind.astype(jnp.int32)
+    greet(barrier)
+    pl.semaphore_wait(barrier, neighbours)
 
     def got(k):
         return step_blocks * (k * parity + (CHUNKS - 1 - k) * (1 - parity))
@@ -173,6 +169,11 @@
             lax.fori_loop(start, start + per_step, lay_out, 0)
         if k >= lag:
             far_pairs(k - lag)
+        if reduce_inside and k < n // 2:
+            if k > 0:
+                pl.semaphore_wait(round_sem.at[k - 1], neighbours)
+            if k < n // 2 - 1:
+                greet(round_sem.at[k])
     first = (me - 1) * blocks
 
     def block_row(at, carry):
@@ -304,6 +305,7 @@
             pltpu.VMEM(final_shape, jnp.float32),
         ] + [dma((CHUNKS,))] * 4 + [dma((LEFT_CHUNKS,))] * 6 + [
             dma((2,)), dma, dma((HALVES, n)), dma((HALVES, n)), dma((HALVES, groups)), dma((HALVES, groups)),
+            pltpu.SemaphoreType.REGULAR((max(n // 2 - 1, 1),)),
         ],
         compiler_params=pltpu.CompilerParams(
             collective_id=0, has_side_effects=True, vmem_limit_bytes=60 * 1024 * 1024

time: 49 us -> 48.7 us (level)
  no operation moved by 1% of the time
where the time goes in v4:
time: 48.7 us; the launch traced here: 48.5 us
  Pallas kernels  46.8 us (96%)
  local copies, waits for them, and re-layouts  1.67 us (3%)
    pallas_call x1, Pallas kernels, local(): pl.pallas_call(functools.partial(kernel, n, groups, reduce_inside), out_s...  46.8 us
    unnamed x1, local copies, waits for them, and re-layouts  1.67 us

profile of v4, /device:TPU:0, one launch (start us, length us, event | category | flops | bytes accessed | tf_op | source)
XLA Modules:
  0.0 48.5 jit_solution(8108149401041236341)
XLA Ops:
  0.0 46.8 %shard_map.55 = f32[4,16,2,512]{3,2,1,0:T(2,128)} custom-call(s32[8,16]{1,0:T(8,128)} %bitcast.3, s32[16]{0:T(128)} %counts_ref.1, bf16[2,16,128,128]{3,2,1,0:T(8,128)(2,1)} %bitcast.2, bf16[2,2048,128]{2,1,0:T(8,128)(2,1)} %left_ref.1, bf16[16,8,2,128,128]{4,3,2,1,0:T(8,128)(2,1)} %dip_ref.1), custom_call_target="tpu_custom_call" | custom-call | tf_op jit(solution)/shard_map/pallas_call | solution.py:290
  46.8 1.7 %copy.7 = f32[4,16,2,512]{3,2,1,0:T(2,128)} copy(f32[4,16,2,512]{3,2,1,0:T(2,128)} %shard_map.55) | data formatting | bytes 524288
